TPU v7x, 32 devices: a whole 2x2x4 slice. The times are simulated.
32 devices in a mesh: mp: 4 (over z), ffn: 8 (over y, x, core).
Axes of the slice: x: 2, y: 2, z: 4, core: 2. Of those that a mesh axis runs over, the one named last changes fastest.
Arguments:
- tokens: bfloat16 [1024, 8192], P('ffn', 'mp'), may hold values from -6 to 6
- gate_weight: bfloat16 [8192, 28672], P('mp', 'ffn'), may hold values from -0.0625 to 0.0625
- up_weight: bfloat16 [8192, 28672], P('mp', 'ffn'), may hold values from -0.0625 to 0.0625
- down_weight: bfloat16 [28672, 8192], P('ffn', 'mp'), may hold values from -0.03125 to 0.03125
Outputs:
- mixed: bfloat16 [1024, 8192], P('ffn', 'mp')
All inputs are finite; a program needn't handle non-finite values.
Results may differ from a plain program's by a relative error of at most 0.03.
Values may be sent and summed in bfloat16 or wider, within the bound.
A program may use at most 128 MiB of HBM per device.

v0:
```python
import jax
import jax.numpy as jnp
from jax import lax
from jax.sharding import PartitionSpec as P


def on_device(tokens, gate_weight, up_weight, down_weight):
    block_rows = lax.all_gather(tokens, "ffn", axis=0, tiled=True)
    gate_part = jnp.dot(block_rows, gate_weight, preferred_element_type=jnp.float32)
    up_part = jnp.dot(block_rows, up_weight, preferred_element_type=jnp.float32)
    partial_terms = jnp.stack((gate_part, up_part), axis=1)
    summed = lax.psum(partial_terms.astype(jnp.bfloat16), "mp").astype(jnp.float32)
    hidden = (jax.nn.silu(summed[:, 0]) * summed[:, 1]).astype(jnp.bfloat16)
    return lax.psum_scatter(
        jnp.dot(hidden, down_weight, preferred_element_type=jnp.float32).astype(jnp.bfloat16),
        "ffn",
        scatter_dimension=0,
        tiled=True,
    )


def solution(mesh):
    in_specs = (P("ffn", "mp"), P("mp", "ffn"), P("mp", "ffn"), P("ffn", "mp"))
    out_specs = P("ffn", "mp")
    return jax.shard_map(
        on_device, mesh=mesh, in_specs=in_specs, out_specs=out_specs, check_vma=False
    )
```

profile of v0, /device:TPU:1, one launch (start us, length us, event | category | flops | bytes accessed | tf_op | source)
XLA Modules:
  0.0 688.7 jit_solution(8396441777294916726)
XLA Ops:
  6.5 0.0 all-gather.2.cloned.1.call-start
  6.5 0.7 all-gather.2.cloned.1.call-update
  7.3 0.0 all-reduce.2.cloned.1.call-start
  7.3 41.2 %all-gather.2.cloned.1.call-done = bf16[1024,2048]{1,0:T(8,128)(2,1)} async-done(((bf16[128,2048]{1,0:T(8,128)(2,1)}), bf16[1024,2048]{1,0:T(8,128)(2,1)}) %all-gather.2.cloned.1.call-update) | async-done | bytes 4194320 | tf_op jit(solution)/shard_map/all_gather | solution.py:8
  48.5 0.0 copy-start
  48.5 21.8 %fusion.5 = bf16[1024,1,3584]{2,0,1:T(8,128)(2,1)S(1)} fusion(bf16[1024,2048]{1,0:T(8,128)(2,1)} %all-gather.2.cloned.1.call-done, bf16[2048,3584]{1,0:T(8,128)(2,1)} %param.6), kind=kOutput, calls=%fused_computation.9 | convolution fusion | flops 15036055552 | bytes 26214400 | tf_op jit(solution)/shard_map/dot_general | solution.py:10
  70.3 0.0 copy-done
  70.3 18.6 %fusion.4 = bf16[1024,1,3584]{2,0,1:T(8,128)(2,1)S(1)} fusion(bf16[1024,2048]{1,0:T(8,128)(2,1)S(1)} %copy-done, bf16[2048,3584]{1,0:T(8,128)(2,1)} %param.5), kind=kOutput, calls=%fused_computation.8 | convolution fusion | flops 15036055552 | bytes 26214400 | tf_op jit(solution)/shard_map/dot_general | solution.py:9
  88.9 6.3 pad_maximum_fusion
  95.2 0.0 all-reduce.2.cloned.1.call-update
  95.2 0.2 reduce-scatter.2.cloned.1.call-start
  95.4 493.3 %all-reduce.2.cloned.1.call-done = bf16[1024,2,3584]{2,0,1:T(8,128)(2,1)} async-done(((bf16[1024,2,3584]{2,0,1:T(8,128)(2,1)}), bf16[1024,2,3584]{2,0,1:T(8,128)(2,1)}) %all-reduce.2.cloned.1.call-update) | async-done | bytes 14680080 | tf_op jit(solution)/shard_map/psum | solution.py:12
  588.7 16.8 %convert_element_type.10 = f32[1024,2,3584]{2,0,1:T(8,128)} convert(bf16[1024,2,3584]{2,0,1:T(8,128)(2,1)} %all-reduce.2.cloned.1.call-done) | non-fusion elementwise | flops 7340032 | bytes 44040192 | tf_op jit(solution)/shard_map/convert_element_type | solution.py:12
  605.5 26.3 %fusion.6 = bf16[1024,2048]{1,0:T(8,128)(2,1)} fusion(bf16[3584,2048]{1,0:T(8,128)(2,1)} %param.7, f32[1024,2,3584]{2,0,1:T(8,128)} %convert_element_type.10), kind=kOutput, calls=%fused_computation.10 | convolution fusion | flops 15056502784 | bytes 48234496 | tf_op jit(solution)/shard_map/dot_general | solution.py:15
  631.8 0.0 reduce-scatter.2.cloned.1.call-update
  631.9 50.4 %reduce-scatter.2.cloned.1.call-done = bf16[128,2048]{1,0:T(8,128)(2,1)} async-done(((bf16[1024,2048]{1,0:T(8,128)(2,1)}), bf16[128,2048]{1,0:T(8,128)(2,1)}) %reduce-scatter.2.cloned.1.call-update) | async-done | bytes 524304 | tf_op jit(solution)/shard_map/reduce_scatter | solution.py:14
Async XLA Ops:
  6.5 42.0 %all-gather.2.cloned.1.call-start = ((), (), s32[]{:S(2)}) async-start(), calls=%async_computation.1 | async-start | bytes 4718592 | tf_op jit(solution)/shard_map/all_gather | solution.py:8
  7.3 581.4 %all-reduce.2.cloned.1.call-start = ((), (), s32[]{:S(2)}) async-start(), calls=%async_computation.2 | async-start | bytes 29360128 | tf_op jit(solution)/shard_map/psum | solution.py:12
  48.5 21.8 %copy-start = (bf16[1024,2048]{1,0:T(8,128)(2,1)S(1)}, bf16[1024,2048]{1,0:T(8,128)(2,1)}, u32[]{:S(2)}) copy-start(bf16[1024,2048]{1,0:T(8,128)(2,1)} %all-gather.2.cloned.1.call-done) | copy-start | bytes 12582916
  95.2 587.0 %reduce-scatter.2.cloned.1.call-start = ((), (), s32[]{:S(2)}) async-start(), calls=%async_computation.3 | async-start | bytes 4718592 | tf_op jit(solution)/shard_map/reduce_scatter | solution.py:14
Sparse Core Ops, SparseCore 0:
  9.2 39.2 all-gather.1
  95.3 493.3 all-reduce.1
  632.0 50.1 reduce-scatter.1
where the time goes:
time: 690 us; the launch traced here: 689 us
  waiting for transfers between devices  586 us (85%)
  matrix products  66.7 us (10%)
  other arithmetic  23.1 us (3%)
  between operations  13.1 us (2%)
    psum x1, waiting for transfers between devices, on_device(): lax.psum(partial_terms.astype(jnp.bfloat16), 'mp').astype(jnp.float32)  493 us
    reduce_scatter x1, waiting for transfers between devices, on_device(): lax.psum_scatter(jnp.dot(hidden, down_weight, preferred_element_type=jnp....  50.4 us
    all_gather x1, waiting for transfers between devices, on_device(): block_rows = lax.all_gather(tokens, 'ffn', axis=0, tiled=True)  41.2 us
    dot_general x1, matrix products, on_device(): jnp.dot(hidden, down_weight, preferred_element_type=jnp.float32)  26.3 us
    dot_general x1, matrix products, on_device(): up_part = jnp.dot(block_rows, up_weight, preferred_element_type=jnp.float32)  21.8 us
    dot_general x1, matrix products, on_device(): jnp.dot(block_rows, gate_weight, preferred_element_type=jnp.float32)  18.6 us
    convert_element_type x1, other arithmetic, on_device(): lax.psum(partial_terms.astype(jnp.bfloat16), 'mp').astype(jnp.float32)  16.8 us
  transfers between devices with their start and end apart: 3, of which 3 were waited for; matrix products, arithmetic and copies ran while one was open for 0% of the time, Pallas kernels for 0%

commit v1 on v0

v1 whole, which is shorter than its diff:
```python
import functools

import jax
import jax.numpy as jnp
from jax import lax
from jax.experimental import pallas as pl
from jax.experimental.pallas import tpu as pltpu
from jax.sharding import PartitionSpec as P

ROWS = 64
SLOTS = 4
MESH = pl.DeviceIdType.MESH


def widest(columns, most=1024):
    return max(w for w in range(128, most + 1, 128) if columns % w == 0)


def xor(a, b, size):
    total, bit = 0, 1
    while bit < size:
        total = total + lax.rem(lax.div(a, bit) + lax.div(b, bit), 2) * bit
        bit *= 2
    return total


def kernel(n, peers, tokens, w_gate, w_up, w_down, out, landed, tok, gate_w, up_w, down_w,
           sum_a, sum_b, part_a, part_b, hid_a, hid_b, mine, outgoing,
           load_sem, tok_send, tok_recv, sum_send, sum_recv, credit, hid_send, hid_recv, out_send, out_recv):
    f32, bf16 = jnp.float32, jnp.bfloat16
    m, f = lax.axis_index("mp"), lax.axis_index("ffn")
    pieces, rows, _ = tokens.shape
    chunks = pieces * peers
    half = sum_a.shape[2] // 2
    width = mine.shape[2]
    last = n - 1
    sums, parts, hids = (sum_a, sum_b), (part_a, part_b), (hid_a, hid_b)
    depths = (m, last - m)
    ahead = (m + 1, m - 1)
    behind = (m - 1, m + 1)

    def turn(p):
        return 1 if p == peers - 1 else p + 1

    gate_load = pltpu.make_async_copy(w_gate, gate_w, load_sem.at[0])
    up_load = pltpu.make_async_copy(w_up, up_w, load_sem.at[1])
    down_load = pltpu.make_async_copy(w_down, down_w, load_sem.at[2])
    own_load = pltpu.make_async_copy(tokens, tok.at[pl.ds(0, pieces)], load_sem.at[3])
    own_load.start()
    gate_load.start()
    up_load.start()

    barrier = pltpu.get_barrier_semaphore()
    for p in range(1, peers):
        pl.semaphore_signal(barrier, inc=1, device_id={"ffn": xor(f, turn(p), peers)}, device_id_type=MESH)

    @pl.when(m > 0)
    def _():
        pl.semaphore_signal(barrier, inc=1, device_id={"mp": m - 1}, device_id_type=MESH)

    @pl.when(m < last)
    def _():
        pl.semaphore_signal(barrier, inc=1, device_id={"mp": m + 1}, device_id_type=MESH)

    pl.semaphore_wait(barrier, peers - 1 + jnp.where(m > 0, 1, 0) + jnp.where(m < last, 1, 0))

    def token_copy(p, peer):
        return pltpu.make_async_remote_copy(
            src_ref=tokens, dst_ref=tok.at[pl.ds(p * pieces, pieces)],
            send_sem=tok_send.at[p], recv_sem=tok_recv.at[p],
            device_id={"ffn": peer}, device_id_type=MESH)

    def sum_copy(d, c):
        slot = lax.rem(c, SLOTS)
        return pltpu.make_async_remote_copy(
            src_ref=sums[d].at[slot], dst_ref=sums[d].at[slot],
            send_sem=sum_send.at[d, lax.rem(c, 2)], recv_sem=sum_recv.at[d, slot],
            device_id={"mp": ahead[d]}, device_id_type=MESH)

    def hid_copy(d, c):
        return pltpu.make_async_remote_copy(
            src_ref=hids[d].at[c], dst_ref=hids[d].at[c],
            send_sem=hid_send.at[d, lax.rem(c, 2)], recv_sem=hid_recv.at[d, c],
            device_id={"mp": behind[d]}, device_id_type=MESH)

    def out_copy(c, peer):
        return pltpu.make_async_remote_copy(
            src_ref=outgoing.at[lax.rem(c, 2)], dst_ref=landed.at[c],
            send_sem=out_send.at[lax.rem(c, 2)], recv_sem=out_recv.at[c],
            device_id={"ffn": peer}, device_id_type=MESH)

    for p in range(1, peers):
        token_copy(p, xor(f, turn(p), peers)).start()
    down_load.start()

    def first_matmul(d, c):
        tile = widest(half)

        @pl.when((c >= 0) & (c < chunks))
        def _():
            @pl.loop(0, half // tile)
            def _(j):
                x = tok[c]
                to = pl.multiple_of(j * tile, tile)
                columns = pl.ds(pl.multiple_of(d * half + j * tile, 128), tile)
                parts[d][:, pl.ds(to, tile)] = jnp.dot(
                    x, gate_w[:, columns], preferred_element_type=f32).astype(bf16)
                parts[d][:, pl.ds(pl.multiple_of(half + j * tile, 128), tile)] = jnp.dot(
                    x, up_w[:, columns], preferred_element_type=f32).astype(bf16)

    def first_matmuls(s):
        q = s - jnp.minimum(depths[0], depths[1])

        @pl.when((q >= pieces) & (q < chunks) & (lax.rem(jnp.maximum(q, 0), pieces) == 0))
        def _():
            token_copy(lax.div(q, pieces), f).wait_recv()

        for d in range(2):
            first_matmul(d, s - depths[d])

    def pass_sum(d, s):
        c = s - depths[d]
        depth, slots, part = depths[d], sums[d], parts[d]

        @pl.when((c >= 0) & (c < chunks))
        def _():
            slot = lax.rem(c, SLOTS)

            @pl.when(depth == 0)
            def _():
                slots[slot] = part[...]

            @pl.when(depth > 0)
            def _():
                sum_copy(d, c).wait_recv()

            @pl.when((depth > 0) & (depth < last))
            def _():
                slots[slot] = (slots[slot].astype(f32) + part[...].astype(f32)).astype(bf16)

            @pl.when(depth < last)
            def _():
                @pl.when(c >= SLOTS)
                def _():
                    pl.semaphore_wait(credit.at[d], 1)

                sum_copy(d, c).start()

            @pl.when(depth == last)
            def _():
                gate = slots[slot, :, :half].astype(f32) + part[:, :half].astype(f32)
                up = slots[slot, :, half:].astype(f32) + part[:, half:].astype(f32)
                hids[d][c] = (gate / (1.0 + jnp.exp(-gate)) * up).astype(bf16)
                hid_copy(d, c).start()

                @pl.when(c + SLOTS < chunks)
                def _():
                    pl.semaphore_signal(credit.at[d], inc=1, device_id={"mp": behind[d]}, device_id_type=MESH)

    def pass_hidden(d, s):
        depth = depths[d]
        c = s - (2 * last - depth)

        @pl.when((depth < last) & (c >= 0) & (c < chunks))
        def _():
            hid_copy(d, c).wait_recv()

            @pl.when(depth > 0)
            def _():
                hid_copy(d, c).start()

    def sent(d, s):
        depth = depths[d]
        c = s - depth - 1

        @pl.when((depth < last) & (c >= 0) & (c < chunks))
        def _():
            sum_copy(d, c).wait_send()

            @pl.when((depth > 0) & (c + SLOTS < chunks))
            def _():
                pl.semaphore_signal(credit.at[d], inc=1, device_id={"mp": behind[d]}, device_id_type=MESH)

        h = s - (2 * last - depth) - 1

        @pl.when((depth > 0) & (h >= 0) & (h < chunks))
        def _():
            hid_copy(d, h).wait_send()

    def second_matmul(s):
        c = s - jnp.maximum(2 * last - m, last + m)
        tile = widest(width)

        def product(j):
            columns = pl.ds(pl.multiple_of(j * tile, tile), tile)
            total = jnp.dot(hid_a[c], down_w[pl.ds(0, half), columns], preferred_element_type=f32)
            total += jnp.dot(hid_b[c], down_w[pl.ds(half, half), columns], preferred_element_type=f32)
            return columns, total.astype(bf16)

        @pl.when(c == 0)
        def _():
            down_load.wait()

        @pl.when((c >= 0) & (c < pieces))
        def _():
            @pl.loop(0, width // tile)
            def _(j):
                columns, total = product(j)
                mine[c, :, columns] = total

        @pl.when((c >= pieces) & (c < chunks))
        def _():
            p = lax.div(c, pieces)
            peer = xor(f, jnp.where(p == peers - 1, 1, p + 1), peers)
            par = lax.rem(c, 2)

            @pl.when(c >= pieces + 2)
            def _():
                out_copy(c, peer).wait_send()

            @pl.loop(0, width // tile)
            def _(j):
                columns, total = product(j)
                outgoing[par, :, columns] = total

            out_copy(c, peer).start()

    own_load.wait()
    gate_load.wait()
    up_load.wait()
    first_matmuls(jnp.int32(0))

    @pl.loop(0, chunks + 2 * last)
    def _(s):
        pass_sum(0, s)
        pass_sum(1, s)
        pass_hidden(0, s)
        pass_hidden(1, s)
        sent(0, s)
        sent(1, s)
        first_matmuls(s + 1)
        second_matmul(s)

    for p in range(1, peers):
        token_copy(p, f).wait_send()
    for c in range(pieces, chunks):
        out_copy(c, f).wait_recv()
        pltpu.make_async_copy(landed.at[c], tok.at[c], out_recv.at[c]).start()
    out[...] = mine[...]
    for c in range(pieces, chunks):
        pltpu.make_async_copy(landed.at[c], tok.at[c], out_recv.at[c]).wait()
    for k in range(pieces):
        total = mine[k].astype(f32)
        for p in range(1, peers):
            total += tok[p * pieces + k].astype(f32)
        out[k] = total.astype(bf16)
    for c in range(chunks - min(2, chunks - pieces), chunks):
        out_copy(c, f).wait_send()


def on_device(n, peers, tokens, gate_weight, up_weight, down_weight):
    held, depth = tokens.shape
    hidden, width = down_weight.shape
    rows, half = ROWS, hidden // 2
    pieces = held // rows
    chunks = pieces * peers
    bf16 = jnp.bfloat16
    dma = pltpu.SemaphoreType.DMA
    flops = 6 * chunks * rows * depth * hidden
    out, _ = pl.pallas_call(
        functools.partial(kernel, n, peers),
        out_shape=(jax.ShapeDtypeStruct((pieces, rows, width), bf16),
                   jax.ShapeDtypeStruct((chunks, rows, width), bf16)),
        in_specs=[pl.BlockSpec(memory_space=pl.ANY)] * 4,
        out_specs=(pl.BlockSpec(memory_space=pltpu.VMEM), pl.BlockSpec(memory_space=pl.ANY)),
        scratch_shapes=[
            pltpu.VMEM((chunks, rows, depth), bf16),
            pltpu.VMEM((depth, hidden), bf16),
            pltpu.VMEM((depth, hidden), bf16),
            pltpu.VMEM((hidden, width), bf16),
            pltpu.VMEM((SLOTS, rows, hidden), bf16),
            pltpu.VMEM((SLOTS, rows, hidden), bf16),
            pltpu.VMEM((rows, hidden), bf16),
            pltpu.VMEM((rows, hidden), bf16),
            pltpu.VMEM((chunks, rows, half), bf16),
            pltpu.VMEM((chunks, rows, half), bf16),
            pltpu.VMEM((pieces, rows, width), bf16),
            pltpu.VMEM((2, rows, width), bf16),
            dma((4,)), dma((peers,)), dma((peers,)), dma((2, 2)), dma((2, SLOTS)),
            pltpu.SemaphoreType.REGULAR((2,)), dma((2, 2)), dma((2, chunks)), dma((2,)), dma((chunks,)),
        ],
        compiler_params=pltpu.CompilerParams(
            collective_id=0, has_side_effects=True, vmem_limit_bytes=63 * 1024 * 1024),
        cost_estimate=pl.CostEstimate(
            flops=flops, bytes_accessed=6 * depth * hidden, transcendentals=chunks * rows * half),
    )(tokens.reshape(pieces, rows, depth), gate_weight, up_weight, down_weight)
    return out.reshape(held, width)


def solution(mesh):
    in_specs = (P("ffn", "mp"), P("mp", "ffn"), P("mp", "ffn"), P("ffn", "mp"))
    body = functools.partial(on_device, mesh.shape["mp"], mesh.shape["ffn"])
    return jax.shard_map(body, mesh=mesh, in_specs=in_specs, out_specs=P("ffn", "mp"), check_vma=False)
```

time: 690 us -> 287 us (0.42)
  waiting for transfers between devices: 586 us -> 0 us
  Pallas kernels: 0 us -> 285 us
  matrix products: 66.7 us -> 0 us
  other arithmetic: 23.1 us -> 0 us
  between operations: 13.1 us -> 0.01 us
    psum x1 -> x0, waiting for transfers between devices: 493 us -> none  [on_device(): lax.psum(partial_terms.astype(jnp.bfloat16), 'mp').astype(jnp.float32)]
    pallas_call x0 -> x1, Pallas kernels: none -> 285 us  [on_device(): pl.pallas_call(functools.partial(kernel, n, peers), out_shape=(jax.ShapeD...]
    dot_general x3 -> x0, matrix products: 66.7 us -> none  [the longest x1 26.3 us: on_device(): jnp.dot(hidden, down_weight, preferred_element_type=jnp.float32)]
    reduce_scatter x1 -> x0, waiting for transfers between devices: 50.4 us -> none  [on_device(): lax.psum_scatter(jnp.dot(hidden, down_weight, preferred_element_type=jnp....]
    all_gather x1 -> x0, waiting for transfers between devices: 41.2 us -> none  [on_device(): block_rows = lax.all_gather(tokens, 'ffn', axis=0, tiled=True)]
    convert_element_type x1 -> x0, other arithmetic: 16.8 us -> none  [on_device(): lax.psum(partial_terms.astype(jnp.bfloat16), 'mp').astype(jnp.float32)]
  transfers between devices with their start and end apart: 3 -> 0, of which waited for: 3 -> 0; matrix products, arithmetic and copies ran while one was open for 0% -> 0% of each run, Pallas kernels for 0% -> 0%
where the time goes in v1:
time: 287 us
  Pallas kernels  285 us (99%)
    pallas_call x1, Pallas kernels, on_device(): pl.pallas_call(functools.partial(kernel, n, peers), out_shape=(jax.ShapeD...  285 us

profile of v1, /device:TPU:1, one launch (start us, length us, event | category | flops | bytes accessed | tf_op | source)
XLA Modules:
  0.0 286.9 jit_solution(14541901860423537477)
XLA Ops:
  0.0 285.0 %shard_map.46 = (bf16[2,64,2048]{2,1,0:T(8,128)(2,1)}, bf16[16,64,2048]{2,1,0:T(8,128)(2,1)}) custom-call(bf16[2,64,2048]{2,1,0:T(8,128)(2,1)} %bitcast.3, bf16[2048,3584]{1,0:T(8,128)(2,1)} %w_gate.1, bf16[2048,3584]{1,0:T(8,128)(2,1)} %w_up.1, bf16[3584,2048]{1,0:T(8,128)(2,1)} %w_down.1), custom_call_target="tpu_custom_call" | custom-call | flops 45097156608 | bytes 44040192 | tf_op jit(solution)/shard_map/pallas_call | solution.py:270
  285.0 1.9 copy.6

commit v2 on v1

v2 whole, which is shorter than its diff:
```python
import functools

import jax
import jax.numpy as jnp
from jax import lax
from jax.experimental import pallas as pl
from jax.experimental.pallas import tpu as pltpu
from jax.sharding import PartitionSpec as P

ROWS = 32
GROUP = 2
SLOTS = 8
MESH = pl.DeviceIdType.MESH


def widest(columns, most=1024):
    return max(w for w in range(128, most + 1, 128) if columns % w == 0)


def xor(a, b, size):
    total, bit = 0, 1
    while bit < size:
        total = total + lax.rem(lax.div(a, bit) + lax.div(b, bit), 2) * bit
        bit *= 2
    return total


def kernel(n, peers, tokens, w_gate, w_up, w_down, out, landed, tok, gate_w, up_w, down_w,
           sum_a, sum_b, part_a, part_b, hid_a, hid_b, mine, outgoing,
           load_sem, tok_send, tok_recv, sum_send, sum_recv, credit, hid_send, hid_recv, out_send, out_recv):
    f32, bf16 = jnp.float32, jnp.bfloat16
    m, f = lax.axis_index("mp"), lax.axis_index("ffn")
    pieces = tokens.shape[0]
    blocks = pieces * peers
    chunks = blocks * GROUP
    half = sum_a.shape[2] // 2
    width = mine.shape[2]
    last = n - 1
    sums, parts, hids = (sum_a, sum_b), (part_a, part_b), (hid_a, hid_b)
    depths = (m, last - m)
    ahead = (m + 1, m - 1)
    behind = (m - 1, m + 1)

    def turn(p):
        return 1 if p == peers - 1 else p + 1

    def half_loads(d):
        columns = pl.ds(d * half, half)
        return (pltpu.make_async_copy(w_gate.at[:, columns], gate_w.at[:, columns], load_sem.at[2 * d]),
                pltpu.make_async_copy(w_up.at[:, columns], up_w.at[:, columns], load_sem.at[2 * d + 1]))

    down_load = pltpu.make_async_copy(w_down, down_w, load_sem.at[4])
    own_load = pltpu.make_async_copy(tokens, tok.at[pl.ds(0, pieces)], load_sem.at[5])
    own_load.start()

    @pl.when(depths[0] <= depths[1])
    def _():
        for load in half_loads(0) + half_loads(1):
            load.start()

    @pl.when(depths[0] > depths[1])
    def _():
        for load in half_loads(1) + half_loads(0):
            load.start()

    barrier = pltpu.get_barrier_semaphore()
    for p in range(1, peers):
        pl.semaphore_signal(barrier, inc=1, device_id={"ffn": xor(f, turn(p), peers)}, device_id_type=MESH)

    @pl.when(m > 0)
    def _():
        pl.semaphore_signal(barrier, inc=1, device_id={"mp": m - 1}, device_id_type=MESH)

    @pl.when(m < last)
    def _():
        pl.semaphore_signal(barrier, inc=1, device_id={"mp": m + 1}, device_id_type=MESH)

    pl.semaphore_wait(barrier, peers - 1 + jnp.where(m > 0, 1, 0) + jnp.where(m < last, 1, 0))

    def block_of(c):
        return lax.div(c, GROUP)

    def rows_of(c):
        return pl.ds(pl.multiple_of(lax.rem(c, GROUP) * ROWS, ROWS), ROWS)

    def token_copy(p, peer):
        return pltpu.make_async_remote_copy(
            src_ref=tokens, dst_ref=tok.at[pl.ds(p * pieces, pieces)],
            send_sem=tok_send.at[p], recv_sem=tok_recv.at[p],
            device_id={"ffn": peer}, device_id_type=MESH)

    def sum_copy(d, c):
        slot = lax.rem(c, SLOTS)
        return pltpu.make_async_remote_copy(
            src_ref=sums[d].at[slot], dst_ref=sums[d].at[slot],
            send_sem=sum_send.at[d, lax.rem(c, 2)], recv_sem=sum_recv.at[d, slot],
            device_id={"mp": ahead[d]}, device_id_type=MESH)

    def hid_copy(d, c):
        return pltpu.make_async_remote_copy(
            src_ref=hids[d].at[block_of(c), rows_of(c)], dst_ref=hids[d].at[block_of(c), rows_of(c)],
            send_sem=hid_send.at[d, lax.rem(c, 2)], recv_sem=hid_recv.at[d, c],
            device_id={"mp": behind[d]}, device_id_type=MESH)

    def out_copy(b, peer):
        return pltpu.make_async_remote_copy(
            src_ref=outgoing.at[lax.rem(b, 2)], dst_ref=landed.at[b],
            send_sem=out_send.at[lax.rem(b, 2)], recv_sem=out_recv.at[b],
            device_id={"ffn": peer}, device_id_type=MESH)

    for p in range(1, peers):
        token_copy(p, xor(f, turn(p), peers)).start()
    down_load.start()

    def first_matmul(d, c):
        tile = widest(half)

        @pl.when(c == 0)
        def _():
            for load in half_loads(d):
                load.wait()

        @pl.when((c >= 0) & (c < chunks) & (lax.rem(jnp.maximum(c, 0), GROUP) == 0))
        def _():
            @pl.loop(0, half // tile)
            def _(j):
                x = tok[block_of(c)]
                to = pl.multiple_of(j * tile, tile)
                columns = pl.ds(pl.multiple_of(d * half + j * tile, 128), tile)
                parts[d][:, pl.ds(to, tile)] = jnp.dot(
                    x, gate_w[:, columns], preferred_element_type=f32).astype(bf16)
                parts[d][:, pl.ds(pl.multiple_of(half + j * tile, 128), tile)] = jnp.dot(
                    x, up_w[:, columns], preferred_element_type=f32).astype(bf16)

    def first_matmuls(s):
        q = s - jnp.minimum(depths[0], depths[1])

        held = pieces * GROUP

        @pl.when((q >= held) & (q < chunks) & (lax.rem(jnp.maximum(q, 0), held) == 0))
        def _():
            token_copy(lax.div(q, held), f).wait_recv()

        for d in range(2):
            first_matmul(d, s - depths[d])

    def pass_sum(d, s):
        c = s - depths[d]
        depth, slots, part = depths[d], sums[d], parts[d]

        @pl.when((c >= 0) & (c < chunks))
        def _():
            slot, own = lax.rem(c, SLOTS), rows_of(c)

            @pl.when(depth == 0)
            def _():
                slots[slot] = part[own, :]

            @pl.when(depth > 0)
            def _():
                sum_copy(d, c).wait_recv()

            @pl.when((depth > 0) & (depth < last))
            def _():
                slots[slot] = (slots[slot].astype(f32) + part[own, :].astype(f32)).astype(bf16)

            @pl.when(depth < last)
            def _():
                @pl.when(c >= SLOTS)
                def _():
                    pl.semaphore_wait(credit.at[d], 1)

                sum_copy(d, c).start()

            @pl.when(depth == last)
            def _():
                gate = slots[slot, :, :half].astype(f32) + part[own, :half].astype(f32)
                up = slots[slot, :, half:].astype(f32) + part[own, half:].astype(f32)
                hids[d][block_of(c), own, :] = (gate / (1.0 + jnp.exp(-gate)) * up).astype(bf16)
                hid_copy(d, c).start()

                @pl.when(c + SLOTS < chunks)
                def _():
                    pl.semaphore_signal(credit.at[d], inc=1, device_id={"mp": behind[d]}, device_id_type=MESH)

    def pass_hidden(d, s):
        depth = depths[d]
        c = s - (2 * last - depth)

        @pl.when((depth < last) & (c >= 0) & (c < chunks))
        def _():
            hid_copy(d, c).wait_recv()

            @pl.when(depth > 0)
            def _():
                hid_copy(d, c).start()

    def sent(d, s):
        depth = depths[d]
        c = s - depth - 1

        @pl.when((depth < last) & (c >= 0) & (c < chunks))
        def _():
            sum_copy(d, c).wait_send()

            @pl.when((depth > 0) & (c + SLOTS < chunks))
            def _():
                pl.semaphore_signal(credit.at[d], inc=1, device_id={"mp": behind[d]}, device_id_type=MESH)

        h = s - (2 * last - depth) - 1

        @pl.when((depth > 0) & (h >= 0) & (h < chunks))
        def _():
            hid_copy(d, h).wait_send()

    def second_matmul(s):
        c = s - jnp.maximum(2 * last - m, last + m) - (GROUP - 1)
        b = block_of(jnp.maximum(c, 0))
        part = lax.rem(jnp.maximum(c, 0), GROUP)
        share = width // GROUP
        tile = widest(share)
        ready = (c >= 0) & (c < chunks)

        def product(j):
            columns = pl.ds(pl.multiple_of(part * share + j * tile, tile), tile)
            total = jnp.dot(hid_a[b], down_w[pl.ds(0, half), columns], preferred_element_type=f32)
            total += jnp.dot(hid_b[b], down_w[pl.ds(half, half), columns], preferred_element_type=f32)
            return columns, total.astype(bf16)

        @pl.when(c == 0)
        def _():
            down_load.wait()

        @pl.when(ready & (b < pieces))
        def _():
            @pl.loop(0, share // tile)
            def _(j):
                columns, total = product(j)
                mine[b, :, columns] = total

        @pl.when(ready & (b >= pieces))
        def _():
            p = lax.div(b, pieces)
            peer = xor(f, jnp.where(p == peers - 1, 1, p + 1), peers)
            par = lax.rem(b, 2)

            @pl.when((b >= pieces + 2) & (part == 0))
            def _():
                out_copy(b, peer).wait_send()

            @pl.loop(0, share // tile)
            def _(j):
                columns, total = product(j)
                outgoing[par, :, columns] = total

            @pl.when(part == GROUP - 1)
            def _():
                out_copy(b, peer).start()

    own_load.wait()
    first_matmuls(jnp.int32(0))

    @pl.loop(0, chunks + 2 * last + GROUP - 1)
    def _(s):
        pass_sum(0, s)
        pass_sum(1, s)
        sent(0, s)
        sent(1, s)
        first_matmuls(s + 1)
        pass_hidden(0, s)
        pass_hidden(1, s)
        second_matmul(s)

    for p in range(1, peers):
        token_copy(p, f).wait_send()
    for b in range(pieces, blocks):
        out_copy(b, f).wait_recv()
        pltpu.make_async_copy(landed.at[b], tok.at[b], out_recv.at[b]).start()
    for b in range(pieces, blocks):
        pltpu.make_async_copy(landed.at[b], tok.at[b], out_recv.at[b]).wait()
    for k in range(pieces):
        total = mine[k].astype(f32)
        for p in range(1, peers):
            total += tok[p * pieces + k].astype(f32)
        out[k] = total.astype(bf16)
    for b in range(blocks - min(2, blocks - pieces), blocks):
        out_copy(b, f).wait_send()


def on_device(n, peers, tokens, gate_weight, up_weight, down_weight):
    held, depth = tokens.shape
    hidden, width = down_weight.shape
    rows, half = ROWS * GROUP, hidden // 2
    pieces = held // rows
    blocks = pieces * peers
    chunks = blocks * GROUP
    bf16 = jnp.bfloat16
    dma = pltpu.SemaphoreType.DMA
    flops = 6 * blocks * rows * depth * hidden
    out, _ = pl.pallas_call(
        functools.partial(kernel, n, peers),
        out_shape=(jax.ShapeDtypeStruct((pieces, rows, width), bf16),
                   jax.ShapeDtypeStruct((blocks, rows, width), bf16)),
        in_specs=[pl.BlockSpec(memory_space=pl.ANY)] * 4,
        out_specs=(pl.BlockSpec(memory_space=pltpu.VMEM), pl.BlockSpec(memory_space=pl.ANY)),
        scratch_shapes=[
            pltpu.VMEM((blocks, rows, depth), bf16),
            pltpu.VMEM((depth, hidden), bf16),
            pltpu.VMEM((depth, hidden), bf16),
            pltpu.VMEM((hidden, width), bf16),
            pltpu.VMEM((SLOTS, ROWS, hidden), bf16),
            pltpu.VMEM((SLOTS, ROWS, hidden), bf16),
            pltpu.VMEM((rows, hidden), bf16),
            pltpu.VMEM((rows, hidden), bf16),
            pltpu.VMEM((blocks, rows, half), bf16),
            pltpu.VMEM((blocks, rows, half), bf16),
            pltpu.VMEM((pieces, rows, width), bf16),
            pltpu.VMEM((2, rows, width), bf16),
            dma((6,)), dma((peers,)), dma((peers,)), dma((2, 2)), dma((2, SLOTS)),
            pltpu.SemaphoreType.REGULAR((2,)), dma((2, 2)), dma((2, chunks)), dma((2,)), dma((blocks,)),
        ],
        compiler_params=pltpu.CompilerParams(
            collective_id=0, has_side_effects=True, vmem_limit_bytes=63 * 1024 * 1024),
        cost_estimate=pl.CostEstimate(
            flops=flops, bytes_accessed=6 * depth * hidden, transcendentals=blocks * rows * half),
    )(tokens.reshape(pieces, rows, depth), gate_weight, up_weight, down_weight)
    return out.reshape(held, width)


def solution(mesh):
    in_specs = (P("ffn", "mp"), P("mp", "ffn"), P("mp", "ffn"), P("ffn", "mp"))
    body = functools.partial(on_device, mesh.shape["mp"], mesh.shape["ffn"])
    return jax.shard_map(body, mesh=mesh, in_specs=in_specs, out_specs=P("ffn", "mp"), check_vma=False)
```

time: 287 us -> 277 us (0.965)
  Pallas kernels: 285 us -> 275 us
    pallas_call x1, Pallas kernels: 285 us -> 275 us  [on_device(): pl.pallas_call(functools.partial(kernel, n, peers), out_shape=(jax.ShapeD...]
where the time goes in v2:
time: 277 us
  Pallas kernels  275 us (99%)
    pallas_call x1, Pallas kernels, on_device(): pl.pallas_call(functools.partial(kernel, n, peers), out_shape=(jax.ShapeD...  275 us

profile of v2, /device:TPU:1, one launch (start us, length us, event | category | flops | bytes accessed | tf_op | source)
XLA Modules:
  0.0 277.3 jit_solution(1021550395744945580)
XLA Ops:
  0.0 275.4 %shard_map.46 = (bf16[2,64,2048]{2,1,0:T(8,128)(2,1)}, bf16[16,64,2048]{2,1,0:T(8,128)(2,1)}) custom-call(bf16[2,64,2048]{2,1,0:T(8,128)(2,1)} %bitcast.3, bf16[2048,3584]{1,0:T(8,128)(2,1)} %w_gate.1, bf16[2048,3584]{1,0:T(8,128)(2,1)} %w_up.1, bf16[3584,2048]{1,0:T(8,128)(2,1)} %w_down.1), custom_call_target="tpu_custom_call" | custom-call | flops 45097156608 | bytes 44040192 | tf_op jit(solution)/shard_map/pallas_call | solution.py:300
  275.4 1.9 copy.6
